TPU v7x, 32 devices: a whole 2x2x4 slice. The times are simulated.
32 devices in a mesh: section: 8 (over y, x, core), tensor: 4 (over z).
Axes of the slice: x: 2, y: 2, z: 4, core: 2. Of those that a mesh axis runs over, the one named last changes fastest.
Arguments:
- fwd_input: bfloat16 [8, 64, 4608], P('section', None, 'tensor'), may hold values from -6 to 6
- bwd_grad: bfloat16 [8, 64, 4608], P('section', None, 'tensor'), may hold values from -6 to 6
- parked: bfloat16 [8, 64, 4608], P('section', None, 'tensor'), may hold values from -6 to 6
- norm_gain: float32 [8, 4608], P('section'), may hold values from 0.25 to 1.75
- w_query: bfloat16 [8, 4608, 512], P('section', None, 'tensor'), may hold values from -1 to 1
- w_key: bfloat16 [8, 4608, 512], P('section', None, 'tensor'), may hold values from -1 to 1
- w_value: bfloat16 [8, 4608, 512], P('section', None, 'tensor'), may hold values from -0.09375 to 0.09375
- w_out: bfloat16 [8, 512, 4608], P('section', 'tensor'), may hold values from -0.25 to 0.25
- offsets: int32 [8, 2, 8], P('section'), may hold values from 0 to 56, as said below
- mirror: int32 [8], replicated, may hold values from 0 to 7, as said below
Outputs:
- next_input: bfloat16 [8, 64, 4608], P('section', None, 'tensor')
- prev_grad: bfloat16 [8, 64, 4608], P('section', None, 'tensor')
- parked_new: bfloat16 [8, 64, 4608], P('section', None, 'tensor')
Inputs may be any that keep to these rules, and one draw needn't show every extreme that they name: Each row offsets[s, j] holds the numbers 0, 8, ..., 56 once each. mirror[t] = t XOR m for one m with 8 / 2 <= m < 8, so sections of the first half pair with sections of the second half.
All inputs are finite; a program needn't handle non-finite values.
Results may differ from a plain program's by a relative error of at most 0.018.
Values may be sent and summed in bfloat16 or wider, within the bound.
A program may use at most 64 MiB of HBM per device.

v0:
```python
import functools

import jax
import jax.numpy as jnp
from jax import lax
from jax.experimental import pallas as pl
from jax.experimental.pallas import tpu as pltpu
from jax.sharding import PartitionSpec as P

HD = 64
SPAN = 8
MESH = pl.DeviceIdType.MESH
F32 = jnp.float32
BF16 = jnp.bfloat16

NN = (((1,), (0,)), ((), ()))
NT = (((1,), (1,)), ((), ()))
TN = (((0,), (0,)), ((), ()))


def dot(a, b, dims):
    return lax.dot_general(a, b, dims, preferred_element_type=F32)


def within(value, size):
    return jnp.logical_and(value >= 0, value < size)


def kernel(
    n_tensor, n_section, n_bits, blocked,
    fwd_ref, grad_ref, park_ref, gain_ref, wq_ref, wk_ref, wv_ref, wo_hbm, offs_ref, mirror_ref,
    next_ref, prev_ref, pnew_ref,
    w, wo, full, part, arrived, acc, stage, zeros, qkv, ssq, dctx, dqkv, got, cur,
    ag_send, ag_recv, rs_send, rs_recv, swap_send, swap_recv, pass_send, pass_recv, local,
):
    t = lax.axis_index("tensor")
    s = lax.axis_index("section")
    rows, width = fwd_ref.shape[1], fwd_ref.shape[2]
    features = width * n_tensor
    cols = wq_ref.shape[2]
    heads = cols // HD
    blocks = offs_ref.shape[2]

    def mate(bit):
        return s + (1 - 2 * ((s // (1 << bit)) % 2)) * (1 << bit)

    barrier = pltpu.get_barrier_semaphore()

    def greet(ok, where):
        @pl.when(ok)
        def _():
            pl.semaphore_signal(barrier, inc=1, device_id=where, device_id_type=MESH)

    greet(t > 0, {"tensor": t - 1})
    greet(t < n_tensor - 1, {"tensor": t + 1})
    greet(s > 0, {"section": s - 1})
    greet(s < n_section - 1, {"section": s + 1})
    for bit in range(n_bits):
        pl.semaphore_signal(barrier, inc=1, device_id={"section": mate(bit)}, device_id_type=MESH)

    loads = [
        pltpu.make_async_copy(fwd_ref.at[0], full.at[0, t], local.at[0]),
        pltpu.make_async_copy(grad_ref.at[0], full.at[1, t], local.at[1]),
        pltpu.make_async_copy(wq_ref.at[0], w.at[:, pl.ds(0, cols)], local.at[2]),
        pltpu.make_async_copy(wk_ref.at[0], w.at[:, pl.ds(cols, cols)], local.at[3]),
        pltpu.make_async_copy(wv_ref.at[0], w.at[:, pl.ds(2 * cols, cols)], local.at[4]),
        pltpu.make_async_copy(wo_hbm if blocked else wo_hbm.at[0], wo, local.at[5]),
    ]
    for load in loads:
        load.start()

    def one(ok):
        return jnp.where(ok, 1, 0)

    pl.semaphore_wait(
        barrier,
        n_bits + one(t > 0) + one(t < n_tensor - 1) + one(s > 0) + one(s < n_section - 1),
    )

    def ag_copy(a, b, way, src):
        return pltpu.make_async_remote_copy(
            src_ref=src, dst_ref=full.at[a, b],
            send_sem=ag_send.at[a, way, b], recv_sem=ag_recv.at[a, b],
            device_id={"tensor": t + 1 - 2 * way}, device_id_type=MESH,
        )

    def ag_own(a, src):
        for way in range(2):
            @pl.when(within(t + 1 - 2 * way, n_tensor))
            def _():
                ag_copy(a, t, way, src).start()

    def ag_round(a, k, consume):
        def step(way, carry):
            b = t + (1 + k) * (2 * way - 1)

            @pl.when(within(b, n_tensor))
            def _():
                ag_copy(a, b, way, full.at[a, b]).wait_recv()

                @pl.when(within(t + 1 - 2 * way, n_tensor))
                def _():
                    ag_copy(a, b, way, full.at[a, b]).start()

                consume(b)

            return carry

        lax.fori_loop(0, 2, step, 0)

    def swap_copy(a, bit):
        if bit == n_bits - 1:
            src = (park_ref if a == 0 else fwd_ref).at[0]
        else:
            src = got.at[a, bit + 1] if bit == n_bits - 2 else cur.at[a, bit + 1]
        return pltpu.make_async_remote_copy(
            src_ref=src, dst_ref=got.at[a, bit],
            send_sem=swap_send.at[a, bit], recv_sem=swap_recv.at[a, bit],
            device_id={"section": mate(bit)}, device_id_type=MESH,
        )

    def swap_finish(a, bit):
        swap_copy(a, bit).wait_recv()
        if bit < n_bits - 1:
            mine = got[a, bit + 1] if bit == n_bits - 2 else cur[a, bit + 1]
            flag = lax.shift_right_logical(mirror_ref[0], bit) & 1
            chosen = jnp.full((rows, width), flag, jnp.int32) == 1
            cur[a, bit] = jnp.where(chosen, got[a, bit].astype(F32), mine.astype(F32)).astype(BF16)
        if bit > 0:
            swap_copy(a, bit - 1).start()

    swap_copy(0, n_bits - 1).start()
    ag_own(0, fwd_ref.at[0])
    ag_own(1, grad_ref.at[0])

    def gain_block(b):
        if blocked:
            return gain_ref[b]
        return gain_ref[0:1, pl.ds(pl.multiple_of(b * width, 128), width)]

    def w_rows(b):
        return w[pl.ds(pl.multiple_of(b * width, 64), width), :]

    def wo_block(b):
        if blocked:
            return wo[b]
        return wo[:, pl.ds(pl.multiple_of(b * width, 128), width)]

    def add_qkv(a, b):
        x = full[a, b].astype(F32)
        ssq[...] += jnp.broadcast_to(jnp.sum(x * x, axis=1, keepdims=True), ssq.shape)
        qkv[...] += dot((x * gain_block(b)).astype(BF16), w_rows(b), NN)

    def add_dctx(b):
        dctx[...] += dot(full[1, b], wo_block(b), NT)

    def clear():
        ssq[...] = jnp.zeros_like(ssq)
        qkv[...] = jnp.zeros_like(qkv)

    clear()
    dctx[...] = jnp.zeros_like(dctx)
    zeros[...] = jnp.zeros_like(zeros)
    for load in loads:
        load.wait()
    add_qkv(0, t)
    add_dctx(t)

    first = [functools.partial(swap_finish, 0, bit) for bit in reversed(range(n_bits))]
    first[0]()

    def round_one(k, carry):
        ag_round(0, k, functools.partial(add_qkv, 0))
        ag_round(1, k, add_dctx)

        @pl.when(k == 0)
        def _():
            for finish in first[1:]:
                finish()
            full[2, t] = cur[0, 0]
            ag_own(2, full.at[2, t])
            swap_copy(1, n_bits - 1).start()

        return carry

    lax.fori_loop(0, n_tensor - 1, round_one, 0)

    lane = lax.broadcasted_iota(jnp.int32, (rows, cols), 1)

    def masked(value):
        return jnp.concatenate(
            [jnp.where(lane // HD == h, value, 0.0) for h in range(heads)], axis=0
        ).astype(BF16)

    def merged(stacked):
        total = stacked[:rows]
        for h in range(1, heads):
            total = jnp.where(lane // HD == h, stacked[h * rows:(h + 1) * rows], total)
        return total

    def places(which, axis):
        index = lax.broadcasted_iota(jnp.int32, (heads * rows, rows), axis) & (rows - 1)
        block = lax.shift_right_logical(index, 3)
        value = index & (SPAN - 1)
        for b in range(blocks):
            value = value + jnp.where(block == b, offs_ref[0, which, b], 0)
        return value

    def attend(which):
        inverse = lax.rsqrt(ssq[:, 0:1] / features + 1e-05)
        scaled = qkv[...] * inverse
        q = masked(scaled[:, :cols])
        k = scaled[:, cols:2 * cols].astype(BF16)
        v = scaled[:, 2 * cols:].astype(BF16)
        scores = dot(q, k, NT) * (HD ** -0.5)
        scores = jnp.where(places(which, 0) >= places(which, 1), scores, -1e30)
        expd = jnp.exp(scores - jnp.max(scores, axis=1, keepdims=True))
        weights = expd / jnp.sum(expd, axis=1, keepdims=True)
        return inverse, q, k, v, weights

    def rs_copy(a, d, way):
        return pltpu.make_async_remote_copy(
            src_ref=part.at[a, d], dst_ref=arrived.at[a, way, d],
            send_sem=rs_send.at[a, d], recv_sem=rs_recv.at[a, way, d],
            device_id={"tensor": t + 1 - 2 * way}, device_id_type=MESH,
        )

    def rs_begin(a, term):
        def step(i, carry):
            d = jnp.where(t < n_tensor // 2, n_tensor - 1 - i, i)
            part[a, d] = term(d).astype(BF16)

            @pl.when(jnp.logical_and(t == 0, d > 0))
            def _():
                rs_copy(a, d, 0).start()

            @pl.when(jnp.logical_and(t == n_tensor - 1, d < n_tensor - 1))
            def _():
                rs_copy(a, d, 1).start()

            return carry

        lax.fori_loop(0, n_tensor, step, 0)
        acc[...] = full[a, t].astype(F32) + part[a, t].astype(F32)

    def rs_round(a, j):
        def step(way, carry):
            d = (1 - way) * (n_tensor - 1 - j) + way * j
            sign = 1 - 2 * way
            ahead = (d - t) * sign

            @pl.when(jnp.logical_and(ahead >= 0, within(t - sign, n_tensor)))
            def _():
                rs_copy(a, d, way).wait_recv()

                @pl.when(ahead > 0)
                def _():
                    part[a, d] = (part[a, d].astype(F32) + arrived[a, way, d].astype(F32)).astype(BF16)
                    rs_copy(a, d, way).start()

                @pl.when(ahead == 0)
                def _():
                    acc[...] += arrived[a, way, d].astype(F32)

            return carry

        lax.fori_loop(0, 2, step, 0)

    def pass_copy(a):
        return pltpu.make_async_remote_copy(
            src_ref=stage.at[a], dst_ref=(next_ref if a == 0 else prev_ref).at[0],
            send_sem=pass_send.at[a], recv_sem=pass_recv.at[a],
            device_id={"section": s + 1 - 2 * a}, device_id_type=MESH,
        )

    def pass_on(a):
        stage[a] = acc[...].astype(BF16)

        @pl.when(within(s + 1 - 2 * a, n_section))
        def _():
            pass_copy(a).start()

    def zero_copy(a):
        return pltpu.make_async_copy(zeros, (next_ref if a == 0 else prev_ref).at[0], local.at[6])

    @pl.when(s == 0)
    def _():
        zero_copy(0).start()

    @pl.when(s == n_section - 1)
    def _():
        zero_copy(1).start()

    inverse, q, k, v, weights = attend(0)
    context = merged(dot(weights.astype(BF16), v, NN)).astype(BF16)
    rs_begin(0, lambda d: dot(context, wo_block(d), NN))
    clear()
    add_qkv(2, t)

    second = [functools.partial(swap_finish, 1, bit) for bit in reversed(range(n_bits))]

    def round_two(k, carry):
        ag_round(2, k, functools.partial(add_qkv, 2))
        rs_round(0, k)

        @pl.when(k == 0)
        def _():
            for finish in second:
                finish()
            pltpu.make_async_copy(cur.at[1, 0], pnew_ref.at[0], local.at[7]).start()

        return carry

    lax.fori_loop(0, n_tensor - 1, round_two, 0)
    pass_on(0)

    inverse, q, k, v, weights = attend(1)
    dc = masked(dctx[...])
    dweights = dot(dc, v, NT)
    dscores = weights * (dweights - jnp.sum(dweights * weights, axis=1, keepdims=True))
    dscores = (dscores * (HD ** -0.5)).astype(BF16)
    dqkv[:, :cols] = merged(dot(dscores, k, NN)).astype(BF16)
    dqkv[:, cols:2 * cols] = dot(dscores, q, TN).astype(BF16)
    dqkv[:, 2 * cols:] = dot(weights.astype(BF16), dc, TN).astype(BF16)
    pull = dqkv[...]
    along = jnp.sum(pull.astype(F32) * qkv[...], axis=1, keepdims=True)
    along = along * inverse * inverse * inverse / features

    def back_term(d):
        dnormed = dot(pull, w_rows(d), NT)
        return inverse * (dnormed * gain_block(d)) - full[2, d].astype(F32) * along

    rs_begin(1, back_term)

    def round_three(j, carry):
        rs_round(1, j)
        return carry

    lax.fori_loop(0, n_tensor - 1, round_three, 0)
    pass_on(1)

    def drain(b, carry):
        for way in range(2):
            sent = (b <= t) if way == 0 else (b >= t)

            @pl.when(jnp.logical_and(sent, within(t + 1 - 2 * way, n_tensor)))
            def _():
                for a in range(3):
                    ag_copy(a, b, way, full.at[a, b]).wait_send()

        @pl.when(b != t)
        def _():
            for a in range(2):
                rs_copy(a, b, 0).wait_send()

        return carry

    lax.fori_loop(0, n_tensor, drain, 0)
    for a in range(2):
        for bit in range(n_bits):
            swap_copy(a, bit).wait_send()
    pltpu.make_async_copy(cur.at[1, 0], pnew_ref.at[0], local.at[7]).wait()
    for a in range(2):
        edge = 0 if a == 0 else n_section - 1

        @pl.when(s == edge)
        def _():
            zero_copy(a).wait()

        @pl.when(s != edge)
        def _():
            pass_copy(a).wait_recv()

        @pl.when(within(s + 1 - 2 * a, n_section))
        def _():
            pass_copy(a).wait_send()


def local_step(n_tensor, n_section, fwd, grad, park, gain, wq, wk, wv, wo, offs, mirror):
    _, rows, width = fwd.shape
    features = gain.shape[1]
    cols = wq.shape[2]
    n_bits = n_section.bit_length() - 1
    blocked = width % 128 != 0
    if blocked:
        gain = gain.reshape(n_tensor, 1, width)
        wo = wo[0].reshape(cols, n_tensor, width).transpose(1, 0, 2)
    heads = cols // HD
    any_spec = pl.BlockSpec(memory_space=pl.ANY)
    vmem = pl.BlockSpec(memory_space=pltpu.VMEM)
    smem = pl.BlockSpec(memory_space=pltpu.SMEM)
    out = jax.ShapeDtypeStruct(fwd.shape, BF16)
    dma = pltpu.SemaphoreType.DMA
    return pl.pallas_call(
        functools.partial(kernel, n_tensor, n_section, n_bits, blocked),
        out_shape=(out, out, out),
        in_specs=[any_spec] * 3 + [vmem] + [any_spec] * 4 + [smem] * 2,
        out_specs=(any_spec,) * 3,
        scratch_shapes=[
            pltpu.VMEM((features, 3 * cols), BF16),
            pltpu.VMEM((n_tensor, cols, width) if blocked else (cols, features), BF16),
            pltpu.VMEM((3, n_tensor, rows, width), BF16),
            pltpu.VMEM((2, n_tensor, rows, width), BF16),
            pltpu.VMEM((2, 2, n_tensor, rows, width), BF16),
            pltpu.VMEM((rows, width), F32),
            pltpu.VMEM((2, rows, width), BF16),
            pltpu.VMEM((rows, width), BF16),
            pltpu.VMEM((rows, 3 * cols), F32),
            pltpu.VMEM((rows, 128), F32),
            pltpu.VMEM((rows, cols), F32),
            pltpu.VMEM((rows, 3 * cols), BF16),
            pltpu.VMEM((2, n_bits, rows, width), BF16),
            pltpu.VMEM((2, n_bits, rows, width), BF16),
            dma((3, 2, n_tensor)),
            dma((3, n_tensor)),
            dma((2, n_tensor)),
            dma((2, 2, n_tensor)),
            dma((2, n_bits)),
            dma((2, n_bits)),
            dma((2,)),
            dma((2,)),
            dma((8,)),
        ],
        compiler_params=pltpu.CompilerParams(
            collective_id=0, has_side_effects=True, vmem_limit_bytes=48 * 1024 * 1024
        ),
    )(fwd, grad, park, gain, wq, wk, wv, wo, offs, mirror)


def solution(mesh):
    in_specs = (
        P("section", None, "tensor"),
        P("section", None, "tensor"),
        P("section", None, "tensor"),
        P("section", None),
        P("section", None, "tensor"),
        P("section", None, "tensor"),
        P("section", None, "tensor"),
        P("section", "tensor", None),
        P("section", None, None),
        P(),
    )
    out_specs = (P("section", None, "tensor"),) * 3
    step = functools.partial(local_step, mesh.shape["tensor"], mesh.shape["section"])
    return jax.shard_map(step, mesh=mesh, in_specs=in_specs, out_specs=out_specs, check_vma=False)
```

profile of v0, /device:TPU:11, one launch (start us, length us, event | category | flops | bytes accessed | tf_op | source)
XLA Modules:
  0.0 96.9 jit_solution(7064814598834639832)
XLA Ops:
  0.6 0.0 copy-start
  0.6 1.3 %copy-done = bf16[1,4608,128]{2,1,0:T(8,128)(2,1)S(1)} copy-done((bf16[1,4608,128]{2,1,0:T(8,128)(2,1)S(1)}, bf16[1,4608,128]{2,1,0:T(8,128)(2,1)}, u32[]{:S(2)}) %copy-start) | copy-done | bytes 1179672
  1.9 0.0 copy-start.1
  1.9 1.3 %copy-done.1 = bf16[1,4608,128]{2,1,0:T(8,128)(2,1)S(1)} copy-done((bf16[1,4608,128]{2,1,0:T(8,128)(2,1)S(1)}, bf16[1,4608,128]{2,1,0:T(8,128)(2,1)}, u32[]{:S(2)}) %copy-start.1) | copy-done | bytes 1179672
  3.2 0.0 copy-start.2
  3.2 1.3 %copy-done.2 = bf16[1,4608,128]{2,1,0:T(8,128)(2,1)S(1)} copy-done((bf16[1,4608,128]{2,1,0:T(8,128)(2,1)S(1)}, bf16[1,4608,128]{2,1,0:T(8,128)(2,1)}, u32[]{:S(2)}) %copy-start.2) | copy-done | bytes 1179672
  4.4 0.0 copy-start.3
  4.5 1.3 %copy-done.3 = bf16[1,128,4608]{2,1,0:T(8,128)(2,1)S(1)} copy-done((bf16[1,128,4608]{2,1,0:T(8,128)(2,1)S(1)}, bf16[1,128,4608]{2,1,0:T(8,128)(2,1)}, u32[]{:S(2)}) %copy-start.3) | copy-done | bytes 1179672
  5.7 0.0 copy-start.4
  5.7 0.9 copy-done.4
  6.6 0.0 copy-start.5
  6.6 0.9 copy-done.5
  7.5 0.0 copy-start.6
  7.5 0.9 copy-done.6
  8.5 0.0 copy-start.7
  8.5 0.7 copy-done.7
  9.2 0.0 copy-start.8
  9.2 0.7 copy-done.8
  9.9 0.0 copy-start.9
  9.9 0.7 copy-done.9
  10.5 84.4 %shard_map.121 = (bf16[1,64,1152]{2,1,0:T(8,128)(2,1)S(1)}, bf16[1,64,1152]{2,1,0:T(8,128)(2,1)S(1)}, bf16[1,64,1152]{2,1,0:T(8,128)(2,1)S(1)}) custom-call(bf16[1,64,1152]{2,1,0:T(8,128)(2,1)S(1)} %copy-done.4, bf16[1,64,1152]{2,1,0:T(8,128)(2,1)S(1)} %copy-done.5, bf16[1,64,1152]{2,1,0:T(8,128)(2,1)S(1)} %copy-done.6, f32[1,4608]{1,0:T(1,128)S(1)} %copy-done.7, ...), custom_call_target="tpu_custom_call" | custom-call | tf_op jit(solution)/shard_map/pallas_call | solution.py:394
  95.0 0.7 copy.16
  95.6 0.7 copy.17
  96.3 0.7 copy.18
Async XLA Ops:
  0.6 1.3 %copy-start = (bf16[1,4608,128]{2,1,0:T(8,128)(2,1)S(1)}, bf16[1,4608,128]{2,1,0:T(8,128)(2,1)}, u32[]{:S(2)}) copy-start(bf16[1,4608,128]{2,1,0:T(8,128)(2,1)} %wq_ref.1) | copy-start | bytes 3538948
  1.9 1.3 %copy-start.1 = (bf16[1,4608,128]{2,1,0:T(8,128)(2,1)S(1)}, bf16[1,4608,128]{2,1,0:T(8,128)(2,1)}, u32[]{:S(2)}) copy-start(bf16[1,4608,128]{2,1,0:T(8,128)(2,1)} %wk_ref.1) | copy-start | bytes 3538948
  3.2 1.3 %copy-start.2 = (bf16[1,4608,128]{2,1,0:T(8,128)(2,1)S(1)}, bf16[1,4608,128]{2,1,0:T(8,128)(2,1)}, u32[]{:S(2)}) copy-start(bf16[1,4608,128]{2,1,0:T(8,128)(2,1)} %wv_ref.1) | copy-start | bytes 3538948
  4.4 1.3 %copy-start.3 = (bf16[1,128,4608]{2,1,0:T(8,128)(2,1)S(1)}, bf16[1,128,4608]{2,1,0:T(8,128)(2,1)}, u32[]{:S(2)}) copy-start(bf16[1,128,4608]{2,1,0:T(8,128)(2,1)} %wo_hbm.1) | copy-start | bytes 3538948
  5.7 0.9 copy-start.4
  6.6 0.9 copy-start.5
  7.5 0.9 copy-start.6
  8.5 0.7 copy-start.7
  9.2 0.7 copy-start.8
  9.9 0.7 copy-start.9
where the time goes:
time: 97.4 us; the launch traced here: 96.9 us
  Pallas kernels  84.4 us (87%)
  local copies, waits for them, and re-layouts  11.8 us (12%)
    pallas_call x1, Pallas kernels, local_step(): pl.pallas_call(functools.partial(kernel, n_tensor, n_section, n_bits, blo...  84.4 us
    unnamed x23, local copies, waits for them, and re-layouts  11.8 us

commit v1 on v0

--- a/solution.py
+++ b/solution.py
@@ -131,7 +131,6 @@
 
     swap_copy(0, n_bits - 1).start()
     ag_own(0, fwd_ref.at[0])
-    ag_own(1, grad_ref.at[0])
 
     def gain_block(b):
         if blocked:
@@ -171,14 +170,16 @@
 
     def round_one(k, carry):
         ag_round(0, k, functools.partial(add_qkv, 0))
-        ag_round(1, k, add_dctx)
 
         @pl.when(k == 0)
+        def _():
+            ag_own(1, grad_ref.at[0])
+
+        @pl.when(k == min(1, n_tensor - 2))
         def _():
             for finish in first[1:]:
                 finish()
             full[2, t] = cur[0, 0]
-            ag_own(2, full.at[2, t])
             swap_copy(1, n_bits - 1).start()
 
         return carry
@@ -229,27 +230,32 @@
         def step(i, carry):
             d = jnp.where(t < n_tensor // 2, n_tensor - 1 - i, i)
             part[a, d] = term(d).astype(BF16)
-
-            @pl.when(jnp.logical_and(t == 0, d > 0))
-            def _():
-                rs_copy(a, d, 0).start()
-
-            @pl.when(jnp.logical_and(t == n_tensor - 1, d < n_tensor - 1))
-            def _():
-                rs_copy(a, d, 1).start()
-
             return carry
 
         lax.fori_loop(0, n_tensor, step, 0)
         acc[...] = full[a, t].astype(F32) + part[a, t].astype(F32)
 
-    def rs_round(a, j):
+    def rs_launch(a, j):
+        for way in range(2):
+            d = n_tensor - 1 - j if way == 0 else j
+
+            @pl.when(t == way * (n_tensor - 1))
+            def _():
+                @pl.when(j > 0)
+                def _():
+                    rs_copy(a, d + 1 - 2 * way, way).wait_send()
+
+                rs_copy(a, d, way).start()
+
+    def rs_tick(a, tick):
         def step(way, carry):
-            d = (1 - way) * (n_tensor - 1 - j) + way * j
+            nth = tick - ((1 - way) * t + way * (n_tensor - 1 - t))
+            d = (1 - way) * (n_tensor - 1 - nth) + way * nth
             sign = 1 - 2 * way
             ahead = (d - t) * sign
-
-            @pl.when(jnp.logical_and(ahead >= 0, within(t - sign, n_tensor)))
+            expected = jnp.logical_and(nth >= 0, ahead >= 0)
+
+            @pl.when(jnp.logical_and(expected, within(t - sign, n_tensor)))
             def _():
                 rs_copy(a, d, way).wait_recv()
 
@@ -294,14 +300,27 @@
     inverse, q, k, v, weights = attend(0)
     context = merged(dot(weights.astype(BF16), v, NN)).astype(BF16)
     rs_begin(0, lambda d: dot(context, wo_block(d), NN))
+
+    def round_two(k, carry):
+        rs_launch(0, k)
+        ag_round(1, k, add_dctx)
+
+        @pl.when(k == 0)
+        def _():
+            ag_own(2, full.at[2, t])
+
+        rs_tick(0, k + 1)
+        return carry
+
+    lax.fori_loop(0, n_tensor - 1, round_two, 0)
+    pass_on(0)
     clear()
     add_qkv(2, t)
 
     second = [functools.partial(swap_finish, 1, bit) for bit in reversed(range(n_bits))]
 
-    def round_two(k, carry):
+    def round_three(k, carry):
         ag_round(2, k, functools.partial(add_qkv, 2))
-        rs_round(0, k)
 
         @pl.when(k == 0)
         def _():
@@ -311,8 +330,7 @@
 
         return carry
 
-    lax.fori_loop(0, n_tensor - 1, round_two, 0)
-    pass_on(0)
+    lax.fori_loop(0, n_tensor - 1, round_three, 0)
 
     inverse, q, k, v, weights = attend(1)
     dc = masked(dctx[...])
@@ -332,11 +350,12 @@
 
     rs_begin(1, back_term)
 
-    def round_three(j, carry):
-        rs_round(1, j)
+    def round_four(j, carry):
+        rs_launch(1, j)
+        rs_tick(1, j + 1)
         return carry
 
-    lax.fori_loop(0, n_tensor - 1, round_three, 0)
+    lax.fori_loop(0, n_tensor - 1, round_four, 0)
     pass_on(1)
 
     def drain(b, carry):
@@ -348,7 +367,9 @@
                 for a in range(3):
                     ag_copy(a, b, way, full.at[a, b]).wait_send()
 
-        @pl.when(b != t)
+        last = jnp.where(t == 0, 1, jnp.where(t == n_tensor - 1, n_tensor - 2, b))
+
+        @pl.when(jnp.logical_and(b != t, b == last))
         def _():
             for a in range(2):
                 rs_copy(a, b, 0).wait_send()
@@ -374,6 +395,11 @@
         @pl.when(within(s + 1 - 2 * a, n_section))
         def _():
             pass_copy(a).wait_send()
+
+
+def hand_over(*refs):
+    for i in range(3):
+        refs[3 + i][...] = refs[i][...]
 
 
 def local_step(n_tensor, n_section, fwd, grad, park, gain, wq, wk, wv, wo, offs, mirror):
@@ -391,7 +417,7 @@
     smem = pl.BlockSpec(memory_space=pltpu.SMEM)
     out = jax.ShapeDtypeStruct(fwd.shape, BF16)
     dma = pltpu.SemaphoreType.DMA
-    return pl.pallas_call(
+    results = pl.pallas_call(
         functools.partial(kernel, n_tensor, n_section, n_bits, blocked),
         out_shape=(out, out, out),
         in_specs=[any_spec] * 3 + [vmem] + [any_spec] * 4 + [smem] * 2,
@@ -422,9 +448,15 @@
             dma((8,)),
         ],
         compiler_params=pltpu.CompilerParams(
-            collective_id=0, has_side_effects=True, vmem_limit_bytes=48 * 1024 * 1024
+            collective_id=0, has_side_effects=True, vmem_limit_bytes=62 * 1024 * 1024
         ),
     )(fwd, grad, park, gain, wq, wk, wv, wo, offs, mirror)
+    return pl.pallas_call(
+        hand_over,
+        out_shape=(out, out, out),
+        in_specs=[vmem] * 3,
+        out_specs=(vmem,) * 3,
+    )(*results)
 
 
 def solution(mesh):

time: 97.4 us -> 74.7 us (0.77)
  local copies, waits for them, and re-layouts: 11.8 us -> 0 us
  Pallas kernels: 84.4 us -> 73.1 us
    pallas_call x1, Pallas kernels: 84.4 us -> 71.2 us  [local_step(): pl.pallas_call(functools.partial(kernel, n_tensor, n_section, n_bits, blo...]
    unnamed x23 -> x0, local copies, waits for them, and re-layouts: 11.8 us -> none
    pallas_call x0 -> x1, Pallas kernels: none -> 1.82 us  [local_step(): pl.pallas_call(hand_over, out_shape=(out, out, out), in_specs=[vmem] * 3,...]
where the time goes in v1:
time: 74.7 us; the launch traced here: 73.7 us
  Pallas kernels  73.1 us (98%)
    pallas_call x1, Pallas kernels, local_step(): pl.pallas_call(functools.partial(kernel, n_tensor, n_section, n_bits, blo...  71.2 us
    pallas_call x1, Pallas kernels, local_step(): pl.pallas_call(hand_over, out_shape=(out, out, out), in_specs=[vmem] * 3,...  1.82 us

profile of v1, /device:TPU:11, one launch (start us, length us, event | category | flops | bytes accessed | tf_op | source)
XLA Modules:
  0.0 73.7 jit_solution(2522397616903333677)
XLA Ops:
  0.6 71.2 %shard_map.121 = (bf16[1,64,1152]{2,1,0:T(8,128)(2,1)}, bf16[1,64,1152]{2,1,0:T(8,128)(2,1)}, bf16[1,64,1152]{2,1,0:T(8,128)(2,1)}) custom-call(bf16[1,64,1152]{2,1,0:T(8,128)(2,1)} %fwd_ref.1, bf16[1,64,1152]{2,1,0:T(8,128)(2,1)} %grad_ref.1, bf16[1,64,1152]{2,1,0:T(8,128)(2,1)} %park_ref.1, f32[1,4608]{1,0:T(1,128)} %gain_ref.1, ...), custom_call_target="tpu_custom_call" | custom-call | tf_op jit(solution)/shard_map/pallas_call | solution.py:420
  71.9 1.8 %shard_map.122 = (bf16[1,64,1152]{2,1,0:T(8,128)(2,1)}, bf16[1,64,1152]{2,1,0:T(8,128)(2,1)}, bf16[1,64,1152]{2,1,0:T(8,128)(2,1)}) custom-call(bf16[1,64,1152]{2,1,0:T(8,128)(2,1)} %get-tuple-element.6.refs_0_, bf16[1,64,1152]{2,1,0:T(8,128)(2,1)} %get-tuple-element.7.refs_1_, bf16[1,64,1152]{2,1,0:T(8,128)(2,1)} %get-tuple-element.8.refs_2_), custom_call_target="tpu_custom_call" | custom-call | tf_op jit(solution)/shard_map/pallas_call | solution.py:454

commit v2 on v1

--- a/solution.py
+++ b/solution.py
@@ -131,6 +131,7 @@
 
     swap_copy(0, n_bits - 1).start()
     ag_own(0, fwd_ref.at[0])
+    ag_own(1, grad_ref.at[0])
 
     def gain_block(b):
         if blocked:
@@ -170,17 +171,16 @@
 
     def round_one(k, carry):
         ag_round(0, k, functools.partial(add_qkv, 0))
-
-        @pl.when(k == 0)
-        def _():
-            ag_own(1, grad_ref.at[0])
-
-        @pl.when(k == min(1, n_tensor - 2))
-        def _():
-            for finish in first[1:]:
-                finish()
-            full[2, t] = cur[0, 0]
-            swap_copy(1, n_bits - 1).start()
+        ag_round(1, k, add_dctx)
+
+        for at in range(n_bits - 1):
+            @pl.when(k == min(at, n_tensor - 2))
+            def _():
+                first[at + 1]()
+                if at == n_bits - 2:
+                    full[2, t] = cur[0, 0]
+                    ag_own(2, full.at[2, t])
+                    swap_copy(1, n_bits - 1).start()
 
         return carry
 
@@ -226,26 +226,30 @@
             device_id={"tensor": t + 1 - 2 * way}, device_id_type=MESH,
         )
 
+    def rs_launch(a, j):
+        for way in range(2):
+            d = n_tensor - 1 - j if way == 0 else j
+
+            @pl.when(t == way * (n_tensor - 1))
+            def _():
+                if not isinstance(j, int):
+                    rs_copy(a, d + 1 - 2 * way, way).wait_send()
+
+                rs_copy(a, d, way).start()
+
     def rs_begin(a, term):
         def step(i, carry):
             d = jnp.where(t < n_tensor // 2, n_tensor - 1 - i, i)
             part[a, d] = term(d).astype(BF16)
+
+            @pl.when(i == 0)
+            def _():
+                rs_launch(a, 0)
+
             return carry
 
         lax.fori_loop(0, n_tensor, step, 0)
         acc[...] = full[a, t].astype(F32) + part[a, t].astype(F32)
-
-    def rs_launch(a, j):
-        for way in range(2):
-            d = n_tensor - 1 - j if way == 0 else j
-
-            @pl.when(t == way * (n_tensor - 1))
-            def _():
-                @pl.when(j > 0)
-                def _():
-                    rs_copy(a, d + 1 - 2 * way, way).wait_send()
-
-                rs_copy(a, d, way).start()
 
     def rs_tick(a, tick):
         def step(way, carry):
@@ -301,36 +305,30 @@
     context = merged(dot(weights.astype(BF16), v, NN)).astype(BF16)
     rs_begin(0, lambda d: dot(context, wo_block(d), NN))
 
-    def round_two(k, carry):
-        rs_launch(0, k)
-        ag_round(1, k, add_dctx)
-
-        @pl.when(k == 0)
-        def _():
-            ag_own(2, full.at[2, t])
-
-        rs_tick(0, k + 1)
-        return carry
-
-    lax.fori_loop(0, n_tensor - 1, round_two, 0)
-    pass_on(0)
     clear()
     add_qkv(2, t)
 
     second = [functools.partial(swap_finish, 1, bit) for bit in reversed(range(n_bits))]
 
     def round_three(k, carry):
+        @pl.when(k > 0)
+        def _():
+            rs_launch(0, k)
+
         ag_round(2, k, functools.partial(add_qkv, 2))
-
-        @pl.when(k == 0)
-        def _():
-            for finish in second:
-                finish()
-            pltpu.make_async_copy(cur.at[1, 0], pnew_ref.at[0], local.at[7]).start()
+        rs_tick(0, k + 1)
+
+        for at in range(n_bits):
+            @pl.when(k == min(at, n_tensor - 2))
+            def _():
+                second[at]()
+                if at == n_bits - 1:
+                    pltpu.make_async_copy(cur.at[1, 0], pnew_ref.at[0], local.at[7]).start()
 
         return carry
 
     lax.fori_loop(0, n_tensor - 1, round_three, 0)
+    pass_on(0)
 
     inverse, q, k, v, weights = attend(1)
     dc = masked(dctx[...])
@@ -351,7 +349,10 @@
     rs_begin(1, back_term)
 
     def round_four(j, carry):
-        rs_launch(1, j)
+        @pl.when(j > 0)
+        def _():
+            rs_launch(1, j)
+
         rs_tick(1, j + 1)
         return carry
 

time: 74.7 us -> 63.7 us (0.85)
  Pallas kernels: 73.1 us -> 61.9 us
    pallas_call x1, Pallas kernels: 71.2 us -> 60 us  [local_step(): pl.pallas_call(functools.partial(kernel, n_tensor, n_section, n_bits, blo...]
where the time goes in v2:
time: 63.7 us; the launch traced here: 62.5 us
  Pallas kernels  61.9 us (97%)
  between operations  0.64 us (1%)
    pallas_call x1, Pallas kernels, local_step(): pl.pallas_call(functools.partial(kernel, n_tensor, n_section, n_bits, blo...  60 us
    pallas_call x1, Pallas kernels, local_step(): pl.pallas_call(hand_over, out_shape=(out, out, out), in_specs=[vmem] * 3,...  1.82 us

profile of v2, /device:TPU:11, one launch (start us, length us, event | category | flops | bytes accessed | tf_op | source)
XLA Modules:
  0.0 62.5 jit_solution(17475602597640680641)
XLA Ops:
  0.6 60.0 %shard_map.121 = (bf16[1,64,1152]{2,1,0:T(8,128)(2,1)}, bf16[1,64,1152]{2,1,0:T(8,128)(2,1)}, bf16[1,64,1152]{2,1,0:T(8,128)(2,1)}) custom-call(bf16[1,64,1152]{2,1,0:T(8,128)(2,1)} %fwd_ref.1, bf16[1,64,1152]{2,1,0:T(8,128)(2,1)} %grad_ref.1, bf16[1,64,1152]{2,1,0:T(8,128)(2,1)} %park_ref.1, f32[1,4608]{1,0:T(1,128)} %gain_ref.1, ...), custom_call_target="tpu_custom_call" | custom-call | tf_op jit(solution)/shard_map/pallas_call | solution.py:421
  60.7 1.8 %shard_map.122 = (bf16[1,64,1152]{2,1,0:T(8,128)(2,1)}, bf16[1,64,1152]{2,1,0:T(8,128)(2,1)}, bf16[1,64,1152]{2,1,0:T(8,128)(2,1)}) custom-call(bf16[1,64,1152]{2,1,0:T(8,128)(2,1)} %get-tuple-element.6.refs_0_, bf16[1,64,1152]{2,1,0:T(8,128)(2,1)} %get-tuple-element.7.refs_1_, bf16[1,64,1152]{2,1,0:T(8,128)(2,1)} %get-tuple-element.8.refs_2_), custom_call_target="tpu_custom_call" | custom-call | tf_op jit(solution)/shard_map/pallas_call | solution.py:455
